TPU v7x, 32 devices: a whole 2x2x4 slice. The times are simulated.
32 devices in a mesh: parts: 2 (over y), row: 4 (over z), col: 4 (over x, core).
Axes of the slice: x: 2, y: 2, z: 4, core: 2. Of those that a mesh axis runs over, the one named last changes fastest.
Arguments:
- normed: bfloat16 [2048, 6144], P(('parts', 'row'), 'col'), parts along dimension 0, may hold values from -6 to 6
- cotangent: bfloat16 [2048, 6144], P(('parts', 'row'), 'col'), parts along dimension 0, may hold values from -6 to 6
- w_up: bfloat16 [6144, 24576], P('col', 'row'), may hold values from -0.078125 to 0.078125
- w_down: bfloat16 [24576, 6144], P('row', 'col'), may hold values from -0.0390625 to 0.0390625
- sign_in_up: int32 [6144, 64], P('col'), may hold values from 0 to 1
- sign_out_up: int32 [24576, 64], P('row'), may hold values from 0 to 1
- sign_in_down: int32 [24576, 64], P('row'), may hold values from 0 to 1
- sign_out_down: int32 [6144, 64], P('col'), may hold values from 0 to 1
- patch_order: int32 [2048], P('parts'), parts along dimension 0, may hold values from 0 to 1023, each once
Outputs:
- sketch_up: float32 [8, 4096], P('parts', ('row', 'col')), parts along dimension 0
- sketch_down: float32 [8, 4096], P('parts', ('row', 'col')), parts along dimension 0
There are 2 independent parts, one for each index of `parts`. A program takes and returns all parts, laid end to end along the dimension named above; an argument that names none is the same for every part. Nothing has to cross between parts.
All inputs are finite; a program needn't handle non-finite values.
Results may differ from a plain program's by a relative error of at most 0.015.
Values may be sent and summed in bfloat16 or wider, within the bound.
No kernel may reach another device: no remote copies, remote signals or barrier semaphores. Data moves between devices by JAX's collectives and lax.ppermute only.
A program may use at most 192 MiB of HBM per device.

v0:
```python
import functools

import jax
import jax.numpy as jnp
from jax import lax
from jax.experimental import pallas as pl
from jax.experimental.pallas import tpu as pltpu
from jax.sharding import PartitionSpec as P

D = 6144
FF = 24576
PATCHES = 256
IMAGES = 4
SCALE = 1.0 / (float(D) * float(FF) * float(PATCHES)) ** 0.5
BF16 = jnp.bfloat16
F32 = jnp.float32


def gelu_terms(pre):
    cdf = 0.5 * (1.0 + lax.erf(pre * 0.7071067811865476))
    pdf = jnp.exp(-0.5 * pre * pre) * 0.3989422804014327
    return pre * cdf, cdf + pre * pdf


def sign_matrix(bits):
    return (2 * bits - 1).astype(BF16)


def members(patch_order):
    images = patch_order // PATCHES
    return (images[None, :] == jnp.arange(IMAGES, dtype=jnp.int32)[:, None]).astype(F32)


def gathered(normed, cotangent, w_up, w_down, sign_in_up, sign_out_up, sign_in_down, sign_out_down, patch_order):
    k = sign_in_up.shape[1]
    x = lax.all_gather(normed, "row", axis=0, tiled=True)
    g = lax.all_gather(cotangent, "row", axis=0, tiled=True)
    up = jnp.dot(x, w_up, preferred_element_type=F32)
    down = lax.dot_general(g, w_down, (((1,), (1,)), ((), ())), preferred_element_type=F32)
    proj = jnp.concatenate(
        [
            jnp.dot(x, sign_matrix(sign_in_up), preferred_element_type=F32),
            jnp.dot(g, sign_matrix(sign_out_down), preferred_element_type=F32),
        ],
        axis=1,
    )
    pre = lax.psum_scatter(up.astype(BF16), "col", scatter_dimension=1, tiled=True).astype(F32)
    back = lax.psum_scatter(down.astype(BF16), "col", scatter_dimension=1, tiled=True).astype(F32)
    proj = lax.psum(proj.astype(BF16), "col").astype(F32)
    units = pre.shape[1]
    first = lax.axis_index("col") * units
    sb = sign_matrix(lax.dynamic_slice_in_dim(sign_out_up, first, units, 0))
    sc = sign_matrix(lax.dynamic_slice_in_dim(sign_in_down, first, units, 0))
    act, slope = gelu_terms(pre)
    side_up = jnp.dot((back * slope).astype(BF16), sb, preferred_element_type=F32)
    side_down = jnp.dot(act.astype(BF16), sc, preferred_element_type=F32)
    table = members(patch_order)
    high = lax.Precision.HIGHEST
    up = jnp.einsum("it,tk,tl->ikl", table, proj[:, :k], side_up, precision=high)
    down = jnp.einsum("it,tk,tl->ikl", table, side_down, proj[:, k:], precision=high)
    return tuple(
        lax.psum_scatter(t.reshape(IMAGES, -1) * SCALE, ("row", "col"), scatter_dimension=1, tiled=True)
        for t in (up, down)
    )


def columns(w_ref, contract, j, tile):
    at = pl.ds(pl.multiple_of(j * tile, tile), tile)
    return w_ref.at[:, at] if contract == 0 else w_ref.at[at, :]


def partial_kernel(contract, tile, pick_ref, order_ref, *refs):
    n = 6 if contract == 0 else 2
    ins, w_ref, refs = refs[:n], refs[n], refs[n + 1 :]
    send_refs, (fwd_ref, keep_ref), refs = refs[:PIECES], refs[PIECES : PIECES + 2], refs[PIECES + 2 :]
    if contract == 0:
        rows, y_ref, w_v, row_sem, w_sem, out_sem, other, bits, other_sem, bits_sem = refs
    else:
        rows, y_ref, w_v, row_sem, w_sem, out_sem = refs
    tiles = w_ref.shape[1 - contract] // tile
    quarter = rows.shape[0] // 4
    piece = 2 * quarter // PIECES
    parts = [(n * piece, piece, ref) for n, ref in enumerate(send_refs)]
    parts += [(2 * quarter, quarter, fwd_ref), (3 * quarter, quarter, keep_ref)]

    def row_copies(source, target, sem):
        return [
            pltpu.make_async_copy(
                source.at[pl.ds(pl.multiple_of(order_ref[j] * quarter, quarter), quarter), :],
                target.at[pl.ds(j * quarter, quarter), :],
                sem.at[j],
            )
            for j in range(4)
        ]

    for choice in (0, 1):

        @pl.when(pick_ref[0] == choice)
        def _():
            for copy in row_copies(ins[choice], rows, row_sem):
                copy.start()

    def load(j):
        return pltpu.make_async_copy(columns(w_ref, contract, j, tile), columns(w_v, contract, j, tile), w_sem.at[j])

    def puts(j, at):
        return [
            pltpu.make_async_copy(y_ref.at[pl.ds(first, count), at], out.at[:, at], out_sem.at[n, j])
            for n, (first, count, out) in enumerate(parts)
        ]

    def span(j):
        return pl.ds(pl.multiple_of(j * tile, tile), tile)

    for j in range(min(AHEAD, tiles)):
        load(j).start()
    for copy in row_copies(ins[0], rows, row_sem):
        copy.wait()
    if contract == 0:
        for choice in (0, 1):

            @pl.when(pick_ref[0] == choice)
            def _():
                for copy in row_copies(ins[2 + choice], other, other_sem):
                    copy.start()

        bit_copies = [pltpu.make_async_copy(ins[4 + n], bits.at[n], bits_sem.at[n]) for n in range(2)]
        for copy in bit_copies:
            copy.start()

    @pl.loop(0, tiles)
    def _(j):
        load(j).wait()

        @pl.when(j + AHEAD < tiles)
        def _():
            load(j + AHEAD).start()

        y_ref[:, span(j)] = lax.dot_general(
            rows[...],
            columns(w_v, contract, j, tile)[...],
            (((1,), (contract,)), ((), ())),
            preferred_element_type=F32,
        ).astype(BF16)
        for copy in puts(j, span(j)):
            copy.start()

    last = []
    if contract == 0:
        for copy in row_copies(ins[2], other, other_sem) + bit_copies:
            copy.wait()
        at = pl.ds(tiles * tile, 2 * bits.shape[1])
        y_ref[:, at] = jnp.concatenate(
            [
                lax.dot_general(
                    left[...], (2 * bits[n] - 1).astype(F32).astype(BF16), ACROSS_DIMS, preferred_element_type=F32
                )
                for n, left in enumerate((rows, other))
            ],
            axis=1,
        ).astype(BF16)
        last = puts(tiles, at)
        for copy in last:
            copy.start()

    @pl.loop(0, tiles)
    def _(j):
        for copy in puts(j, span(j)):
            copy.wait()

    for copy in last:
        copy.wait()


ACROSS_DIMS = (((1,), (1,)), ((), ()))
COST = 4.8e9
ECOST = 2.6e9
AHEAD = 3
PIECES = 4


def in_hbm(*arrays):
    return [pltpu.with_memory_space_constraint(a, pltpu.HBM) for a in arrays]


def partial_product(pick, order, x, w, contract, g=None, bits=None):
    tokens, depth = x[0].shape
    units = w.shape[1 - contract]
    tile = 1024 if units % 1024 == 0 else units
    tiles = units // tile
    quarter = tokens // 4
    anywhere = pl.BlockSpec(memory_space=pl.ANY)
    scalars = pl.BlockSpec(memory_space=pltpu.SMEM)
    ins, scratch, width = [*x], [], units
    if g is not None:
        ins += [*g, *bits]
        width += 2 * bits[0].shape[0]
        scratch = [
            pltpu.VMEM((tokens, depth), BF16),
            pltpu.VMEM((2, *bits[0].shape), bits[0].dtype),
            pltpu.SemaphoreType.DMA((4,)),
            pltpu.SemaphoreType.DMA((2,)),
        ]
    ins = in_hbm(*ins, w)
    return pl.pallas_call(
        functools.partial(partial_kernel, contract, tile),
        in_specs=[scalars, scalars] + [anywhere] * len(ins),
        out_specs=[anywhere] * (PIECES + 2),
        out_shape=[pltpu.HBM((2 * quarter // PIECES, width), BF16)] * PIECES
        + [pltpu.VMEM((quarter, width), BF16), pltpu.HBM((quarter, width), BF16)],
        scratch_shapes=[
            pltpu.VMEM((tokens, depth), BF16),
            pltpu.VMEM((tokens, width), BF16),
            pltpu.VMEM(w.shape, BF16),
            pltpu.SemaphoreType.DMA((4,)),
            pltpu.SemaphoreType.DMA((tiles,)),
            pltpu.SemaphoreType.DMA((PIECES + 2, tiles + 1)),
        ]
        + scratch,
        compiler_params=pltpu.CompilerParams(vmem_limit_bytes=36 * 2**20),
        cost_estimate=pl.CostEstimate(flops=int(COST), bytes_accessed=1000, transcendentals=0),
    )(pick, order, *ins)


def add_kernel(a_ref, *refs):
    terms, (out_ref, slots, sems) = refs[:-3], refs[-3:]
    piece = terms[0].shape[0]
    copies = [pltpu.make_async_copy(a_ref, slots.at[0], sems.at[0])]
    for n, ref in enumerate(terms):
        copies.append(pltpu.make_async_copy(ref, slots.at[1, pl.ds(n * piece, piece), :], sems.at[1 + n]))
    for copy in copies:
        copy.start()
    for copy in copies:
        copy.wait()
    out_ref[...] = (slots[0].astype(F32) + slots[1].astype(F32)).astype(BF16)


def add_rows(a, b):
    return pl.pallas_call(
        add_kernel,
        in_specs=[pl.BlockSpec(memory_space=pl.ANY)] * (1 + len(b)),
        out_specs=pl.BlockSpec(memory_space=pltpu.VMEM),
        out_shape=jax.ShapeDtypeStruct(a.shape, BF16),
        scratch_shapes=[pltpu.VMEM((2, *a.shape), BF16), pltpu.SemaphoreType.DMA((1 + len(b),))],
        compiler_params=pltpu.CompilerParams(vmem_limit_bytes=16 * 2**20),
        cost_estimate=pl.CostEstimate(flops=1000, bytes_accessed=1000, transcendentals=0),
    )(pltpu.with_memory_space_constraint(a, pltpu.VMEM), *b)


def gathered_terms(refs, slots, sems):
    piece = refs[2].shape[0]
    copies = [
        pltpu.make_async_copy(refs[0], slots.at[0], sems.at[0]),
        pltpu.make_async_copy(refs[1], slots.at[1], sems.at[1]),
    ]
    for n, ref in enumerate(refs[2:]):
        copies.append(pltpu.make_async_copy(ref, slots.at[2, pl.ds(n * piece, piece), :], sems.at[2 + n]))
    for copy in copies:
        copy.start()
    return copies


def total(slots, at):
    return slots[0, :, at].astype(F32) + slots[1, :, at].astype(F32) + slots[2, :, at].astype(F32)


def over_chunks(units, body, init):
    chunk = 1024 if units % 1024 == 0 else units
    return lax.fori_loop(0, units // chunk, lambda j, c: body(pl.ds(pl.multiple_of(j * chunk, chunk), chunk), c), init)


def act_kernel(n, *refs):
    terms, (sc, down_ref, slope_ref, proj_ref, slots, sems) = refs[:n], refs[n:]
    for copy in gathered_terms(terms, slots, sems):
        copy.wait()
    units = slope_ref.shape[1]

    def body(at, side):
        act, slope = gelu_terms(total(slots, at))
        slope_ref[:, at] = slope
        return side + lax.dot_general(act.astype(BF16), sc[:, at], ACROSS_DIMS, preferred_element_type=F32)

    down_ref[...] = over_chunks(units, body, jnp.zeros(down_ref.shape, F32))
    proj_ref[...] = total(slots, pl.ds(units, proj_ref.shape[1]))


def back_kernel(n, *refs):
    terms, (slope_ref, sb, up_ref, slots, sems) = refs[:n], refs[n:]
    for copy in gathered_terms(terms, slots, sems):
        copy.wait()

    def body(at, side):
        dpre = (total(slots, at) * slope_ref[:, at]).astype(BF16)
        return side + lax.dot_general(dpre, sb[:, at], ACROSS_DIMS, preferred_element_type=F32)

    up_ref[...] = over_chunks(slope_ref.shape[1], body, jnp.zeros(up_ref.shape, F32))


def sides_kernel(n, steps, *refs):
    terms = refs[: 2 * n * steps]
    b_ref, c_ref, up_ref, down_ref, proj_ref, sb, sc, ups, downs, bits, sems, bit_sems = refs[2 * n * steps :]
    quarter, units = downs.shape[2:]
    bit_copies = [
        pltpu.make_async_copy(b_ref, bits.at[0], bit_sems.at[0]),
        pltpu.make_async_copy(c_ref, bits.at[1], bit_sems.at[1]),
    ]
    for copy in bit_copies:
        copy.start()

    def fetch(s):
        up, down = terms[2 * n * s : 2 * n * s + n], terms[2 * n * s + n : 2 * n * s + 2 * n]
        return gathered_terms(up, ups.at[s % 2], sems.at[s, 0]) + gathered_terms(down, downs.at[s % 2], sems.at[s, 1])

    coming = fetch(0)
    for copy in bit_copies:
        copy.wait()
    sb[...] = (2 * bits[0] - 1).astype(F32).astype(BF16)
    sc[...] = (2 * bits[1] - 1).astype(F32).astype(BF16)
    for s in range(steps):
        for copy in coming:
            copy.wait()
        if s + 1 < steps:
            coming = fetch(s + 1)

        def body(at, both):
            act, slope = gelu_terms(total(ups.at[s % 2], at))
            dpre = (total(downs.at[s % 2], at) * slope).astype(BF16)
            return (
                both[0] + lax.dot_general(dpre, sb[:, at], ACROSS_DIMS, preferred_element_type=F32),
                both[1] + lax.dot_general(act.astype(BF16), sc[:, at], ACROSS_DIMS, preferred_element_type=F32),
            )

        zeros = jnp.zeros((quarter, up_ref.shape[1]), F32)
        side_up, side_down = over_chunks(units, body, (zeros, zeros))
        mine = slice(s * quarter, (s + 1) * quarter)
        up_ref[mine] = side_up
        down_ref[mine] = side_down
        proj_ref[mine] = total(ups.at[s % 2], pl.ds(units, proj_ref.shape[1]))


def side_call(kernel, terms, others, outs, scratch, cost):
    vmem, anywhere = pl.BlockSpec(memory_space=pltpu.VMEM), pl.BlockSpec(memory_space=pl.ANY)
    others, in_vmem = zip(*others)
    return pl.pallas_call(
        kernel,
        in_specs=[anywhere] * len(terms) + [vmem if v else anywhere for v in in_vmem],
        out_specs=[vmem] * len(outs),
        out_shape=outs,
        scratch_shapes=scratch,
        compiler_params=pltpu.CompilerParams(vmem_limit_bytes=24 * 2**20),
        cost_estimate=pl.CostEstimate(flops=int(cost), bytes_accessed=1000, transcendentals=0),
    )(*in_hbm(*terms), *others)


SIBLING = [(0, 1), (1, 0), (2, 3), (3, 2)]
ACROSS = [(0, 2), (2, 0), (1, 3), (3, 1)]


def pipelined(normed, cotangent, w_up, w_down, sign_in_up, sign_out_up, sign_in_down, sign_out_down, patch_order):
    k = sign_in_up.shape[1]
    col = lax.axis_index("col")
    row = lax.axis_index("row")
    shard = normed.shape[0]
    quarter = shard // 4
    order = jnp.stack([3 - col, col ^ 1, col ^ 2, col]).astype(jnp.int32)
    inner = (row == 1) | (row == 2)

    def hop(a, pairs):
        return lax.ppermute(a, "row", pairs)

    def tie(a, *others):
        return lax.optimization_barrier((a, *others))[0]

    zero = jnp.zeros((1,), jnp.int32)
    pick = jnp.where(inner, 0, 1).astype(jnp.int32).reshape(1)
    PAIRS, MIDDLE, OUTER = [(0, 1), (1, 0), (2, 3), (3, 2)], [(1, 2), (2, 1)], [(1, 0), (2, 3)]
    sources = [row, row ^ 1, jnp.where(row < 2, 2, 1), jnp.where(row < 2, 3, 0)]
    weights = (w_up, w_down)
    bits = (sign_in_up.T, sign_out_down.T)
    shards = [normed, cotangent]
    products, received, outs, far = [], [], [], []

    def product(i, p, x, g, *after):
        if after:
            p = tie(p, *after)
        extra = (g, bits) if i % 2 == 0 else ()
        products.append(partial_product(p, order, g if i % 2 else x, weights[i % 2], i % 2, *extra))
        received.append([lax.ppermute(send, "col", SIBLING) for send in products[i][:PIECES]])

    def combine(i, after=None):
        got = received[i]
        if after is not None:
            got = tie(got, after)
        half = PIECES // 2
        outs.append((add_rows(products[i][PIECES], got[:half]), got[half:]))
        far.append(lax.ppermute(outs[i][0], "col", ACROSS))

    def terms(i):
        return (products[i][PIECES + 1], far[i], *outs[i][1])

    x, g = shards
    x1, x2 = hop(x, PAIRS), hop(x, MIDDLE)
    product(0, zero, (x, x), (g, g))
    combine(0)
    product(1, zero, (x, x), (g, g), outs[0][0], x1, x2)
    g1, g2 = hop(g, PAIRS), hop(g, MIDDLE)
    combine(1)
    product(2, zero, (x1, x1), (g1, g1), outs[1][0], far[0], g1, g2)
    x2b, x3 = hop(x2, OUTER), hop(tie(x1, products[1][0]), MIDDLE)
    combine(2)
    product(3, zero, (x1, x1), (g1, g1), outs[2][0], far[1], x2b, x3)
    g2b, g3 = hop(g2, OUTER), hop(tie(g1, products[2][0]), MIDDLE)
    combine(3)
    product(4, pick, (x2, x2b), (g2, g2b), outs[3][0], far[2], g2b, g3)
    x3b = hop(tie(x3, products[3][0]), OUTER)
    combine(4)
    product(5, pick, (x2, x2b), (g2, g2b), outs[4][0], far[3], x3b)
    g3b = hop(tie(g3, products[4][0]), OUTER)
    combine(5)
    product(6, pick, (x3, x3b), (g3, g3b), outs[5][0], far[4], g3b)
    combine(6)
    product(7, pick, (x3, x3b), (g3, g3b), outs[6][0], far[5])
    combine(7, far[6])
    n, units = len(terms(0)), w_up.shape[1]
    b, c = tie((sign_out_up, sign_in_down), outs[7][0])
    early = 3 * quarter
    sides_up, sides_down, projs, sb, sc = side_call(
        functools.partial(sides_kernel, n, 3),
        [t for i in range(6) for t in terms(i)],
        [(b.T, False), (c.T, False)],
        [jax.ShapeDtypeStruct((early, k), F32)] * 2
        + [jax.ShapeDtypeStruct((early, 2 * k), F32)]
        + [jax.ShapeDtypeStruct((k, units), BF16)] * 2,
        [
            pltpu.VMEM((2, 3, quarter, units + 2 * k), BF16),
            pltpu.VMEM((2, 3, quarter, units), BF16),
            pltpu.VMEM((2, k, units), jnp.int32),
            pltpu.SemaphoreType.DMA((3, 2, n)),
            pltpu.SemaphoreType.DMA((2,)),
        ],
        1000,
    )
    down, slope, last = side_call(
        functools.partial(act_kernel, n),
        terms(6),
        [(sc, True)],
        [
            jax.ShapeDtypeStruct((quarter, k), F32),
            jax.ShapeDtypeStruct((quarter, units), F32),
            jax.ShapeDtypeStruct((quarter, 2 * k), F32),
        ],
        [pltpu.VMEM((3, quarter, units + 2 * k), BF16), pltpu.SemaphoreType.DMA((n,))],
        ECOST,
    )
    up = side_call(
        functools.partial(back_kernel, n),
        terms(7),
        [(slope, True), (sb, True)],
        [jax.ShapeDtypeStruct((quarter, k), F32)],
        [pltpu.VMEM((3, quarter, units), BF16), pltpu.SemaphoreType.DMA((n,))],
        1000,
    )[0]
    side_up = jnp.concatenate([sides_up, up])
    side_down = jnp.concatenate([sides_down, down])
    proj = jnp.concatenate([projs, last])

    table = members(patch_order)
    tables = [
        lax.dynamic_slice_in_dim(table, sources[s] * shard + col * quarter, quarter, 1) for s in range(4)
    ]
    table = jnp.concatenate(tables, axis=1)
    high = lax.Precision.HIGHEST
    up = jnp.einsum("it,tk,tl->ikl", table, proj[:, :k], side_up, precision=high)
    down = jnp.einsum("it,tk,tl->ikl", table, side_down, proj[:, k:], precision=high)
    both = jnp.stack([up.reshape(IMAGES, 4, 4, -1), down.reshape(IMAGES, 4, 4, -1)]) * SCALE
    both = both.transpose(2, 3, 0, 1, 4)

    both = both.reshape(4, 2, 2, *both.shape[2:])
    chip, core = col // 2, col % 2
    mine = lax.dynamic_index_in_dim(both, chip, 1, keepdims=False)
    theirs = lax.dynamic_index_in_dim(both, 1 - chip, 1, keepdims=False)
    both = mine + lax.ppermute(theirs, "col", ACROSS)
    mine = lax.dynamic_index_in_dim(both, core, 1, keepdims=False)
    theirs = lax.dynamic_index_in_dim(both, 1 - core, 1, keepdims=False)
    both = mine + lax.ppermute(theirs, "col", SIBLING)
    total = lax.dynamic_index_in_dim(both, row, 0, keepdims=False)
    for off in (1, 2, 3):
        block = lax.dynamic_index_in_dim(both, row ^ off, 0, keepdims=False)
        total = total + hop(block, [(i, i ^ off) for i in range(4)])
    return total[0], total[1]


def solution(mesh):
    line = mesh.shape["row"] == 4 and mesh.shape["col"] == 4
    in_specs = (
        P(("parts", "row"), "col"),
        P(("parts", "row"), "col"),
        P("col", "row"),
        P("row", "col"),
        P("col", None),
        P("row", None),
        P("row", None),
        P("col", None),
        P("parts"),
    )
    out_specs = (P("parts", ("row", "col")), P("parts", ("row", "col")))
    return jax.shard_map(
        pipelined if line else gathered, mesh=mesh, in_specs=in_specs, out_specs=out_specs, check_vma=False
    )
```

profile of v0, /device:TPU:0, one launch (start us, length us, event | category | flops | bytes accessed | tf_op | source)
XLA Modules:
  0.0 200.7 jit_solution(2077914835940699980)
XLA Ops:
  0.6 3.1 %collective-permute-start.5 = (bf16[256,1536]{1,0:T(8,128)(2,1)}, bf16[256,1536]{1,0:T(8,128)(2,1)S(1)}, u32[]{:S(2)}, u32[]{:S(2)}) collective-permute-start(bf16[256,1536]{1,0:T(8,128)(2,1)} %refs_1_.2), channel_id=1, source_target_pairs={{0,4},{4,0},{8,12},{12,8},{1,5},{5,1},{9,13},{13,9},{2,6},{6,2},{1... | collective-permute-start | bytes 2359304 | tf_op jit(solution)/shard_map/ppermute | solution.py:369
  4.5 11.4 %shard_map.104 = (bf16[32,6272]{1,0:T(8,128)(2,1)}, bf16[32,6272]{1,0:T(8,128)(2,1)}, bf16[32,6272]{1,0:T(8,128)(2,1)}, bf16[32,6272]{1,0:T(8,128)(2,1)}, bf16[6...) custom-call(s32[1]{0:T(128)} %constant.67.clone.1.pick_ref, s32[4]{0:T(128)S(1)} %pad_add_fusion.order_ref, ...), custom_call_target="tpu_custom_call" | custom-call | flops 4800000000 | bytes 1000 | tf_op jit(solution)/shard_map/pallas_call | solution.py:205
  16.5 4.3 %collective-permute-start.12 = (bf16[256,1536]{1,0:T(8,128)(2,1)S(1)}, bf16[256,1536]{1,0:T(8,128)(2,1)S(1)}, u32[]{:S(2)}, u32[]{:S(2)}) collective-permute-start(bf16[256,1536]{1,0:T(8,128)(2,1)S(1)} %copy-done.6), channel_id=1, source_target_pairs={{0,4},{4,0},{8,12},{12,8},{1,5},{5,1},{9,13},{13,9},{2,6},{6,2},{1... | collective-permute-start | bytes 2359304 | tf_op jit(solution)/shard_map/ppermute | solution.py:369
  20.8 1.6 collective-permute-start.13
  23.1 1.6 collective-permute-start.2
  24.6 10.3 %shard_map.106 = (bf16[32,6144]{1,0:T(8,128)(2,1)}, bf16[32,6144]{1,0:T(8,128)(2,1)}, bf16[32,6144]{1,0:T(8,128)(2,1)}, bf16[32,6144]{1,0:T(8,128)(2,1)}, bf16[6...) custom-call(s32[1]{0:T(128)} %constant.67.clone.1.pick_ref, s32[4]{0:T(128)S(1)} %pad_add_fusion.order_ref, ...), custom_call_target="tpu_custom_call" | custom-call | flops 4800000000 | bytes 1000 | tf_op jit(solution)/shard_map/pallas_call | solution.py:205
  40.2 2.7 %collective-permute-done.2.refs_1_ = bf16[64,6272]{1,0:T(8,128)(2,1)S(1)} collective-permute-done((bf16[64,6272]{1,0:T(8,128)(2,1)S(1)}, bf16[64,6272]{1,0:T(8,128)(2,1)S(1)}, u32[]{:S(2)}, u32[]{:S(2)}) %collective-permute-start.2) | collective-permute-done | bytes 802848 | tf_op jit(solution)/shard_map/ppermute | solution.py:396
  43.0 11.4 %shard_map.108 = (bf16[32,6272]{1,0:T(8,128)(2,1)}, bf16[32,6272]{1,0:T(8,128)(2,1)}, bf16[32,6272]{1,0:T(8,128)(2,1)}, bf16[32,6272]{1,0:T(8,128)(2,1)}, bf16[6...) custom-call(s32[1]{0:T(128)} %constant.67.clone.1.pick_ref, s32[4]{0:T(128)S(1)} %pad_add_fusion.order_ref, ...), custom_call_target="tpu_custom_call" | custom-call | flops 4800000000 | bytes 1000 | tf_op jit(solution)/shard_map/pallas_call | solution.py:205
  57.7 1.5 collective-permute-start.27
  59.9 1.9 collective-permute-done.19.refs_1_
  63.3 10.3 %shard_map.110 = (bf16[32,6144]{1,0:T(8,128)(2,1)}, bf16[32,6144]{1,0:T(8,128)(2,1)}, bf16[32,6144]{1,0:T(8,128)(2,1)}, bf16[32,6144]{1,0:T(8,128)(2,1)}, bf16[6...) custom-call(s32[1]{0:T(128)} %constant.67.clone.1.pick_ref, s32[4]{0:T(128)S(1)} %pad_add_fusion.order_ref, ...), custom_call_target="tpu_custom_call" | custom-call | flops 4800000000 | bytes 1000 | tf_op jit(solution)/shard_map/pallas_call | solution.py:205
  79.4 2.1 %collective-permute-done.16.refs_9_ = bf16[64,6272]{1,0:T(8,128)(2,1)} collective-permute-done((bf16[64,6272]{1,0:T(8,128)(2,1)S(1)}, bf16[64,6272]{1,0:T(8,128)(2,1)}, u32[]{:S(2)}, u32[]{:S(2)}) %collective-permute-start.16) | collective-permute-done | bytes 802848 | tf_op jit(solution)/shard_map/ppermute | solution.py:396
  81.5 11.4 %shard_map.112 = (bf16[32,6272]{1,0:T(8,128)(2,1)}, bf16[32,6272]{1,0:T(8,128)(2,1)}, bf16[32,6272]{1,0:T(8,128)(2,1)}, bf16[32,6272]{1,0:T(8,128)(2,1)}, bf16[6...) custom-call(s32[1]{0:T(128)} %bitcast.6.pick_ref, s32[4]{0:T(128)S(1)} %pad_add_fusion.order_ref, ...), custom_call_target="tpu_custom_call" | custom-call | flops 4800000000 | bytes 1000 | tf_op jit(solution)/shard_map/pallas_call | solution.py:205
  96.2 2.5 %collective-permute-start.30 = (bf16[64,6272]{1,0:T(8,128)(2,1)S(1)}, bf16[64,6272]{1,0:T(8,128)(2,1)S(1)}, u32[]{:S(2)}, u32[]{:S(2)}) collective-permute-start(bf16[64,6272]{1,0:T(8,128)(2,1)S(1)} %shard_map.113), channel_id=1, source_target_pairs={{0,2},{2,0},{1,3},{3,1},{4,6},{6,4},{5,7},{7,5},{8,10},{10,8},{9,1... | collective-permute-start | bytes 2408456 | tf_op jit(solution)/shard_map/ppermute | solution.py:396
  98.7 11.0 %shard_map.114 = (bf16[32,6144]{1,0:T(8,128)(2,1)}, bf16[32,6144]{1,0:T(8,128)(2,1)}, bf16[32,6144]{1,0:T(8,128)(2,1)}, bf16[32,6144]{1,0:T(8,128)(2,1)}, bf16[6...) custom-call(s32[1]{0:T(128)} %bitcast.6.pick_ref, s32[4]{0:T(128)S(1)} %pad_add_fusion.order_ref, ...), custom_call_target="tpu_custom_call" | custom-call | flops 4800000000 | bytes 1000 | tf_op jit(solution)/shard_map/pallas_call | solution.py:205
  113.6 3.4 %collective-permute-done.39.refs_3_.refs_1_ = bf16[256,1536]{1,0:T(8,128)(2,1)S(1)} collective-permute-done((bf16[256,1536]{1,0:T(8,128)(2,1)}, bf16[256,1536]{1,0:T(8,128)(2,1)S(1)}, u32[]{:S(2)}, u32[]{:S(2)}) %collective-permute-start.39) | collective-permute-done | bytes 786464 | tf_op jit(solution)/shard_map/ppermute | solution.py:369
  117.9 11.5 %shard_map.116 = (bf16[32,6272]{1,0:T(8,128)(2,1)}, bf16[32,6272]{1,0:T(8,128)(2,1)}, bf16[32,6272]{1,0:T(8,128)(2,1)}, bf16[32,6272]{1,0:T(8,128)(2,1)}, bf16[6...) custom-call(s32[1]{0:T(128)} %bitcast.6.pick_ref, s32[4]{0:T(128)S(1)} %pad_add_fusion.order_ref, ...), custom_call_target="tpu_custom_call" | custom-call | flops 4800000000 | bytes 1000 | tf_op jit(solution)/shard_map/pallas_call | solution.py:205
  133.8 1.6 shard_map.117
  138.1 1.7 collective-permute-start.46
  139.9 11.0 %shard_map.118 = (bf16[32,6144]{1,0:T(8,128)(2,1)}, bf16[32,6144]{1,0:T(8,128)(2,1)}, bf16[32,6144]{1,0:T(8,128)(2,1)}, bf16[32,6144]{1,0:T(8,128)(2,1)}, bf16[6...) custom-call(s32[1]{0:T(128)} %bitcast.6.pick_ref, s32[4]{0:T(128)S(1)} %pad_add_fusion.order_ref, ...), custom_call_target="tpu_custom_call" | custom-call | flops 4800000000 | bytes 1000 | tf_op jit(solution)/shard_map/pallas_call | solution.py:205
  156.5 1.8 collective-permute-done.46.refs_1_
  159.6 2.3 %shard_map.119 = bf16[64,6144]{1,0:T(8,128)(2,1)} custom-call(bf16[64,6144]{1,0:T(8,128)(2,1)S(1)} %copy-done.5, bf16[32,6144]{1,0:T(8,128)(2,1)S(1)} %collective-permute-done.42.refs_0_, bf16[32,6144]{1,0:T(8,128)(2,1)} %collective-permute-done.43.refs_1_), custom_call_target="tpu_custom_call" | custom-call | flops 1000 | bytes 1000 | tf_op jit(solution)/shard_map/pallas_call | solution.py:239
  161.9 1.8 collective-permute-start.49
  164.7 9.8 %shard_map.120 = (f32[192,64]{1,0:T(8,128)S(1)}, f32[192,64]{1,0:T(8,128)S(1)}, f32[192,128]{1,0:T(8,128)S(1)}, bf16[64,6144]{1,0:T(8,128)(2,1)S(1)}, bf16[64,6144]{1,0:T(8,128)(2,1)S(1)}) custom-call(bf16[64,6272]{1,0:T(8,128)(2,1)} %get-tuple-element.75.refs_0_, bf16[64,6272]{1,0:T(8,128)(2,1)} %copy-done.10, bf16[32,6272]{1,0:T(8,128)(2,1)} %copy-done.19, ...), custom_call_target="tpu_custom_call" | custom-call | flops 1000 | bytes 1000 | tf_op jit(solution)/shard_map/pallas_call | solution.py:344
  175.5 3.3 %shard_map.121 = (f32[64,64]{1,0:T(8,128)S(1)}, f32[64,6144]{1,0:T(8,128)S(1)}, f32[64,128]{1,0:T(8,128)S(1)}) custom-call(bf16[64,6272]{1,0:T(8,128)(2,1)} %get-tuple-element.135.refs_0_, bf16[64,6272]{1,0:T(8,128)(2,1)} %collective-permute-done.46.refs_1_, bf16[32,6272]{1,0:T(8,128)(2,1)} %copy-done.34, bf16[32,6272]{1,0:T(8,128)(2,1)} %copy-done.35, ...), custom_call_target="tpu_custom_call" | custom-call | flops 2600000000 | bytes 1000 | tf_op jit(solution)/shard_map/pallas_call | solution.py:344
  179.6 2.6 %collective-permute-done.49.refs_1_ = bf16[64,6144]{1,0:T(8,128)(2,1)} collective-permute-done((bf16[64,6144]{1,0:T(8,128)(2,1)}, bf16[64,6144]{1,0:T(8,128)(2,1)}, u32[]{:S(2)}, u32[]{:S(2)}) %collective-permute-start.49) | collective-permute-done | bytes 786464 | tf_op jit(solution)/shard_map/ppermute | solution.py:396
  182.3 2.8 %shard_map.122 = f32[64,64]{1,0:T(8,128)S(1)} custom-call(bf16[64,6144]{1,0:T(8,128)(2,1)} %get-tuple-element.141.refs_0_, bf16[64,6144]{1,0:T(8,128)(2,1)} %collective-permute-done.49.refs_1_, bf16[32,6144]{1,0:T(8,128)(2,1)} %collective-permute-done.44.refs_2_, bf16[32,6144]{1,0:T(8,128)(2,1)} %collective-permute-done.45.refs_3_, ...), custom_call_target="tpu_custom_call" | custom-call | flops 1000 | bytes 1000 | tf_op jit(solution)/shard_map/pallas_call | solution.py:344
  185.7 1.8 collective-permute-start.50
  187.5 2.5 %collective-permute-done.50 = f32[4,2,2,4,256]{4,3,2,1,0:T(4,128)S(1)} collective-permute-done((f32[4,2,2,4,256]{4,3,2,1,0:T(4,128)S(1)}, f32[4,2,2,4,256]{4,3,2,1,0:T(4,128)S(1)}, u32[]{:S(2)}, u32[]{:S(2)}) %collective-permute-start.50) | collective-permute-done | bytes 65568 | tf_op jit(solution)/shard_map/ppermute | solution.py:482
  191.4 2.1 %collective-permute-start.54 = (f32[2,4,256]{2,1,0:T(4,128)S(1)}, f32[2,4,256]{2,1,0:T(4,128)S(1)}, u32[]{:S(2)}, u32[]{:S(2)}) collective-permute-start(f32[2,4,256]{2,1,0:T(4,128)S(1)} %get-tuple-element.149), channel_id=1, source_target_pairs={{0,12},{4,8},{8,4},{12,0},{1,13},{5,9},{9,5},{13,1},{2,14},{6,10},... | collective-permute-start | bytes 24584 | tf_op jit(solution)/shard_map/ppermute | solution.py:369
  193.5 3.0 %collective-permute-start.53 = (f32[2,4,256]{2,1,0:T(4,128)S(1)}, f32[2,4,256]{2,1,0:T(4,128)S(1)}, u32[]{:S(2)}, u32[]{:S(2)}) collective-permute-start(f32[2,4,256]{2,1,0:T(4,128)S(1)} %get-tuple-element.150), channel_id=1, source_target_pairs={{0,8},{4,12},{8,0},{12,4},{1,9},{5,13},{9,1},{13,5},{2,10},{6,14},... | collective-permute-start | bytes 24584 | tf_op jit(solution)/shard_map/ppermute | solution.py:369
  198.2 1.9 collective-permute-done.52
  (201 shorter events, 47.2 us)
Async XLA Ops:
  0.6 24.0 %collective-permute-start.5 = (bf16[256,1536]{1,0:T(8,128)(2,1)}, bf16[256,1536]{1,0:T(8,128)(2,1)S(1)}, u32[]{:S(2)}, u32[]{:S(2)}) collective-permute-start(bf16[256,1536]{1,0:T(8,128)(2,1)} %refs_1_.2), channel_id=1, source_target_pairs={{0,4},{4,0},{8,12},{12,8},{1,5},{5,1},{9,13},{13,9},{2,6},{6,2},{1... | collective-permute-start | bytes 2359304 | tf_op jit(solution)/shard_map/ppermute | solution.py:369
  3.7 20.9 %collective-permute-start.6 = (bf16[256,1536]{1,0:T(8,128)(2,1)}, bf16[256,1536]{1,0:T(8,128)(2,1)S(1)}, u32[]{:S(2)}, u32[]{:S(2)}) collective-permute-start(bf16[256,1536]{1,0:T(8,128)(2,1)} %refs_1_.2), channel_id=1, source_target_pairs={{4,8},{8,4},{5,9},{9,5},{6,10},{10,6},{7,11},{11,7},{20,24},{24,20... | collective-permute-start | bytes 2359304 | tf_op jit(solution)/shard_map/ppermute | solution.py:369
  16.0 6.4 %collective-permute-start.1 = (bf16[32,6272]{1,0:T(8,128)(2,1)}, bf16[32,6272]{1,0:T(8,128)(2,1)S(1)}, u32[]{:S(2)}, u32[]{:S(2)}) collective-permute-start(bf16[32,6272]{1,0:T(8,128)(2,1)} %get-tuple-element.78), channel_id=1, source_target_pairs={{0,1},{1,0},{2,3},{3,2},{4,5},{5,4},{6,7},{7,6},{8,9},{9,8},{10,11... | collective-permute-start | bytes 1204232 | tf_op jit(solution)/shard_map/ppermute | solution.py:388
  16.5 23.2 %collective-permute-start.12 = (bf16[256,1536]{1,0:T(8,128)(2,1)S(1)}, bf16[256,1536]{1,0:T(8,128)(2,1)S(1)}, u32[]{:S(2)}, u32[]{:S(2)}) collective-permute-start(bf16[256,1536]{1,0:T(8,128)(2,1)S(1)} %copy-done.6), channel_id=1, source_target_pairs={{0,4},{4,0},{8,12},{12,8},{1,5},{5,1},{9,13},{13,9},{2,6},{6,2},{1... | collective-permute-start | bytes 2359304 | tf_op jit(solution)/shard_map/ppermute | solution.py:369
  20.8 19.4 %collective-permute-start.13 = (bf16[256,1536]{1,0:T(8,128)(2,1)S(1)}, bf16[256,1536]{1,0:T(8,128)(2,1)}, u32[]{:S(2)}, u32[]{:S(2)}) collective-permute-start(bf16[256,1536]{1,0:T(8,128)(2,1)S(1)} %copy-done.6), channel_id=1, source_target_pairs={{4,8},{8,4},{5,9},{9,5},{6,10},{10,6},{7,11},{11,7},{20,24},{24,20... | collective-permute-start | bytes 2359304 | tf_op jit(solution)/shard_map/ppermute | solution.py:369
  23.1 19.9 %collective-permute-start.2 = (bf16[64,6272]{1,0:T(8,128)(2,1)S(1)}, bf16[64,6272]{1,0:T(8,128)(2,1)S(1)}, u32[]{:S(2)}, u32[]{:S(2)}) collective-permute-start(bf16[64,6272]{1,0:T(8,128)(2,1)S(1)} %shard_map.105), channel_id=1, source_target_pairs={{0,2},{2,0},{1,3},{3,1},{4,6},{6,4},{5,7},{7,5},{8,10},{10,8},{9,1... | collective-permute-start | bytes 2408456 | tf_op jit(solution)/shard_map/ppermute | solution.py:396
  36.9 26.3 %collective-permute-start.20 = (bf16[256,1536]{1,0:T(8,128)(2,1)S(1)}, bf16[256,1536]{1,0:T(8,128)(2,1)S(1)}, u32[]{:S(2)}, u32[]{:S(2)}) collective-permute-start(bf16[256,1536]{1,0:T(8,128)(2,1)S(1)} %collective-permute-done.5.refs_0_.refs_1_), channel_id=1, source_target_pairs={{4,8},{8,4},{5,9},{9,5},{6,10},{10,6},{7,11},{11,7},{20,24},{24,20... | collective-permute-start | bytes 2359304 | tf_op jit(solution)/shard_map/ppermute | solution.py:369
  37.7 24.1 %collective-permute-start.19 = (bf16[256,1536]{1,0:T(8,128)(2,1)S(1)}, bf16[256,1536]{1,0:T(8,128)(2,1)S(1)}, u32[]{:S(2)}, u32[]{:S(2)}) collective-permute-start(bf16[256,1536]{1,0:T(8,128)(2,1)S(1)} %collective-permute-done.6.refs_0_), channel_id=1, source_target_pairs={{4,0},{8,12},{5,1},{9,13},{6,2},{10,14},{7,3},{11,15},{20,16},{24,... | collective-permute-start | bytes 2359304 | tf_op jit(solution)/shard_map/ppermute | solution.py:369
  39.6 23.6 %collective-permute-start.9 = (bf16[64,6144]{1,0:T(8,128)(2,1)S(1)}, bf16[64,6144]{1,0:T(8,128)(2,1)S(1)}, u32[]{:S(2)}, u32[]{:S(2)}) collective-permute-start(bf16[64,6144]{1,0:T(8,128)(2,1)S(1)} %shard_map.107), channel_id=1, source_target_pairs={{0,2},{2,0},{1,3},{3,1},{4,6},{6,4},{5,7},{7,5},{8,10},{10,8},{9,1... | collective-permute-start | bytes 2359304 | tf_op jit(solution)/shard_map/ppermute | solution.py:396
  56.4 23.0 %collective-permute-start.26 = (bf16[256,1536]{1,0:T(8,128)(2,1)}, bf16[256,1536]{1,0:T(8,128)(2,1)}, u32[]{:S(2)}, u32[]{:S(2)}) collective-permute-start(bf16[256,1536]{1,0:T(8,128)(2,1)} %collective-permute-done.13.refs_2_.refs_0_), channel_id=1, source_target_pairs={{4,0},{8,12},{5,1},{9,13},{6,2},{10,14},{7,3},{11,15},{20,16},{24,... | collective-permute-start | bytes 2359304 | tf_op jit(solution)/shard_map/ppermute | solution.py:369
  57.7 21.7 %collective-permute-start.27 = (bf16[256,1536]{1,0:T(8,128)(2,1)}, bf16[256,1536]{1,0:T(8,128)(2,1)}, u32[]{:S(2)}, u32[]{:S(2)}) collective-permute-start(bf16[256,1536]{1,0:T(8,128)(2,1)} %copy-done.7), channel_id=1, source_target_pairs={{4,8},{8,4},{5,9},{9,5},{6,10},{10,6},{7,11},{11,7},{20,24},{24,20... | collective-permute-start | bytes 2359304 | tf_op jit(solution)/shard_map/ppermute | solution.py:369
  61.8 19.7 %collective-permute-start.16 = (bf16[64,6272]{1,0:T(8,128)(2,1)S(1)}, bf16[64,6272]{1,0:T(8,128)(2,1)}, u32[]{:S(2)}, u32[]{:S(2)}) collective-permute-start(bf16[64,6272]{1,0:T(8,128)(2,1)S(1)} %shard_map.109), channel_id=1, source_target_pairs={{0,2},{2,0},{1,3},{3,1},{4,6},{6,4},{5,7},{7,5},{8,10},{10,8},{9,1... | collective-permute-start | bytes 2408456 | tf_op jit(solution)/shard_map/ppermute | solution.py:396
  75.6 23.1 %collective-permute-start.33 = (bf16[256,1536]{1,0:T(8,128)(2,1)}, bf16[256,1536]{1,0:T(8,128)(2,1)S(1)}, u32[]{:S(2)}, u32[]{:S(2)}) collective-permute-start(bf16[256,1536]{1,0:T(8,128)(2,1)} %copy-done.15), channel_id=1, source_target_pairs={{4,0},{8,12},{5,1},{9,13},{6,2},{10,14},{7,3},{11,15},{20,16},{24,... | collective-permute-start | bytes 2359304 | tf_op jit(solution)/shard_map/ppermute | solution.py:369
  77.5 21.2 %collective-permute-start.23 = (bf16[64,6144]{1,0:T(8,128)(2,1)S(1)}, bf16[64,6144]{1,0:T(8,128)(2,1)S(1)}, u32[]{:S(2)}, u32[]{:S(2)}) collective-permute-start(bf16[64,6144]{1,0:T(8,128)(2,1)S(1)} %shard_map.111), channel_id=1, source_target_pairs={{0,2},{2,0},{1,3},{3,1},{4,6},{6,4},{5,7},{7,5},{8,10},{10,8},{9,1... | collective-permute-start | bytes 2359304 | tf_op jit(solution)/shard_map/ppermute | solution.py:396
  93.5 23.5 %collective-permute-start.39 = (bf16[256,1536]{1,0:T(8,128)(2,1)}, bf16[256,1536]{1,0:T(8,128)(2,1)S(1)}, u32[]{:S(2)}, u32[]{:S(2)}) collective-permute-start(bf16[256,1536]{1,0:T(8,128)(2,1)} %collective-permute-done.27.refs_2_.refs_0_), channel_id=1, source_target_pairs={{4,0},{8,12},{5,1},{9,13},{6,2},{10,14},{7,3},{11,15},{20,16},{24,... | collective-permute-start | bytes 2359304 | tf_op jit(solution)/shard_map/ppermute | solution.py:369
  96.2 21.2 %collective-permute-start.30 = (bf16[64,6272]{1,0:T(8,128)(2,1)S(1)}, bf16[64,6272]{1,0:T(8,128)(2,1)S(1)}, u32[]{:S(2)}, u32[]{:S(2)}) collective-permute-start(bf16[64,6272]{1,0:T(8,128)(2,1)S(1)} %shard_map.113), channel_id=1, source_target_pairs={{0,2},{2,0},{1,3},{3,1},{4,6},{6,4},{5,7},{7,5},{8,10},{10,8},{9,1... | collective-permute-start | bytes 2408456 | tf_op jit(solution)/shard_map/ppermute | solution.py:396
  113.0 20.7 %collective-permute-start.36 = (bf16[64,6144]{1,0:T(8,128)(2,1)S(1)}, bf16[64,6144]{1,0:T(8,128)(2,1)S(1)}, u32[]{:S(2)}, u32[]{:S(2)}) collective-permute-start(bf16[64,6144]{1,0:T(8,128)(2,1)S(1)} %shard_map.115), channel_id=1, source_target_pairs={{0,2},{2,0},{1,3},{3,1},{4,6},{6,4},{5,7},{7,5},{8,10},{10,8},{9,1... | collective-permute-start | bytes 2359304 | tf_op jit(solution)/shard_map/ppermute | solution.py:396
  130.0 5.4 %collective-permute-start.3 = (bf16[32,6272]{1,0:T(8,128)(2,1)S(1)}, bf16[32,6272]{1,0:T(8,128)(2,1)S(1)}, u32[]{:S(2)}, u32[]{:S(2)}) collective-permute-start(bf16[32,6272]{1,0:T(8,128)(2,1)S(1)} %copy-done.30), channel_id=1, source_target_pairs={{0,1},{1,0},{2,3},{3,2},{4,5},{5,4},{6,7},{7,6},{8,9},{9,8},{10,11... | collective-permute-start | bytes 1204232 | tf_op jit(solution)/shard_map/ppermute | solution.py:388
  130.1 5.9 %collective-permute-start.4 = (bf16[32,6272]{1,0:T(8,128)(2,1)S(1)}, bf16[32,6272]{1,0:T(8,128)(2,1)S(1)}, u32[]{:S(2)}, u32[]{:S(2)}) collective-permute-start(bf16[32,6272]{1,0:T(8,128)(2,1)S(1)} %copy-done.29), channel_id=1, source_target_pairs={{0,1},{1,0},{2,3},{3,2},{4,5},{5,4},{6,7},{7,6},{8,9},{9,8},{10,11... | collective-permute-start | bytes 1204232 | tf_op jit(solution)/shard_map/ppermute | solution.py:388
  131.4 5.3 %collective-permute-start.17 = (bf16[32,6272]{1,0:T(8,128)(2,1)S(1)}, bf16[32,6272]{1,0:T(8,128)(2,1)S(1)}, u32[]{:S(2)}, u32[]{:S(2)}) collective-permute-start(bf16[32,6272]{1,0:T(8,128)(2,1)S(1)} %copy-done.32), channel_id=1, source_target_pairs={{0,1},{1,0},{2,3},{3,2},{4,5},{5,4},{6,7},{7,6},{8,9},{9,8},{10,11... | collective-permute-start | bytes 1204232 | tf_op jit(solution)/shard_map/ppermute | solution.py:388
  135.4 16.4 %collective-permute-start.18 = (bf16[32,6272]{1,0:T(8,128)(2,1)S(1)}, bf16[32,6272]{1,0:T(8,128)(2,1)S(1)}, u32[]{:S(2)}, u32[]{:S(2)}) collective-permute-start(bf16[32,6272]{1,0:T(8,128)(2,1)S(1)} %copy-done.31), channel_id=1, source_target_pairs={{0,1},{1,0},{2,3},{3,2},{4,5},{5,4},{6,7},{7,6},{8,9},{9,8},{10,11... | collective-permute-start | bytes 1204232 | tf_op jit(solution)/shard_map/ppermute | solution.py:388
  136.0 16.6 %collective-permute-start.24 = (bf16[32,6144]{1,0:T(8,128)(2,1)S(1)}, bf16[32,6144]{1,0:T(8,128)(2,1)}, u32[]{:S(2)}, u32[]{:S(2)}) collective-permute-start(bf16[32,6144]{1,0:T(8,128)(2,1)S(1)} %copy-done.39), channel_id=1, source_target_pairs={{0,1},{1,0},{2,3},{3,2},{4,5},{5,4},{6,7},{7,6},{8,9},{9,8},{10,11... | collective-permute-start | bytes 1179656 | tf_op jit(solution)/shard_map/ppermute | solution.py:388
  136.1 17.0 %collective-permute-start.25 = (bf16[32,6144]{1,0:T(8,128)(2,1)S(1)}, bf16[32,6144]{1,0:T(8,128)(2,1)}, u32[]{:S(2)}, u32[]{:S(2)}) collective-permute-start(bf16[32,6144]{1,0:T(8,128)(2,1)S(1)} %copy-done.38), channel_id=1, source_target_pairs={{0,1},{1,0},{2,3},{3,2},{4,5},{5,4},{6,7},{7,6},{8,9},{9,8},{10,11... | collective-permute-start | bytes 1179656 | tf_op jit(solution)/shard_map/ppermute | solution.py:388
  136.6 16.5 %collective-permute-start.31 = (bf16[32,6272]{1,0:T(8,128)(2,1)S(1)}, bf16[32,6272]{1,0:T(8,128)(2,1)}, u32[]{:S(2)}, u32[]{:S(2)}) collective-permute-start(bf16[32,6272]{1,0:T(8,128)(2,1)S(1)} %copy-done.33), channel_id=1, source_target_pairs={{0,1},{1,0},{2,3},{3,2},{4,5},{5,4},{6,7},{7,6},{8,9},{9,8},{10,11... | collective-permute-start | bytes 1204232 | tf_op jit(solution)/shard_map/ppermute | solution.py:388
  138.1 20.2 %collective-permute-start.46 = (bf16[64,6272]{1,0:T(8,128)(2,1)}, bf16[64,6272]{1,0:T(8,128)(2,1)}, u32[]{:S(2)}, u32[]{:S(2)}) collective-permute-start(bf16[64,6272]{1,0:T(8,128)(2,1)} %shard_map.117), channel_id=1, source_target_pairs={{0,2},{2,0},{1,3},{3,1},{4,6},{6,4},{5,7},{7,5},{8,10},{10,8},{9,1... | collective-permute-start | bytes 2408456 | tf_op jit(solution)/shard_map/ppermute | solution.py:396
  155.0 7.0 %collective-permute-start.32 = (bf16[32,6272]{1,0:T(8,128)(2,1)}, bf16[32,6272]{1,0:T(8,128)(2,1)S(1)}, u32[]{:S(2)}, u32[]{:S(2)}) collective-permute-start(bf16[32,6272]{1,0:T(8,128)(2,1)} %get-tuple-element.110), channel_id=1, source_target_pairs={{0,1},{1,0},{2,3},{3,2},{4,5},{5,4},{6,7},{7,6},{8,9},{9,8},{10,11... | collective-permute-start | bytes 1204232 | tf_op jit(solution)/shard_map/ppermute | solution.py:388
  155.2 8.6 %collective-permute-start.37 = (bf16[32,6144]{1,0:T(8,128)(2,1)}, bf16[32,6144]{1,0:T(8,128)(2,1)S(1)}, u32[]{:S(2)}, u32[]{:S(2)}) collective-permute-start(bf16[32,6144]{1,0:T(8,128)(2,1)} %get-tuple-element.117), channel_id=1, source_target_pairs={{0,1},{1,0},{2,3},{3,2},{4,5},{5,4},{6,7},{7,6},{8,9},{9,8},{10,11... | collective-permute-start | bytes 1179656 | tf_op jit(solution)/shard_map/ppermute | solution.py:388
  155.8 8.0 %collective-permute-start.38 = (bf16[32,6144]{1,0:T(8,128)(2,1)}, bf16[32,6144]{1,0:T(8,128)(2,1)S(1)}, u32[]{:S(2)}, u32[]{:S(2)}) collective-permute-start(bf16[32,6144]{1,0:T(8,128)(2,1)} %get-tuple-element.118), channel_id=1, source_target_pairs={{0,1},{1,0},{2,3},{3,2},{4,5},{5,4},{6,7},{7,6},{8,9},{9,8},{10,11... | collective-permute-start | bytes 1179656 | tf_op jit(solution)/shard_map/ppermute | solution.py:388
  156.3 18.1 %collective-permute-start.47 = (bf16[32,6272]{1,0:T(8,128)(2,1)}, bf16[32,6272]{1,0:T(8,128)(2,1)S(1)}, u32[]{:S(2)}, u32[]{:S(2)}) collective-permute-start(bf16[32,6272]{1,0:T(8,128)(2,1)} %get-tuple-element.136), channel_id=1, source_target_pairs={{0,1},{1,0},{2,3},{3,2},{4,5},{5,4},{6,7},{7,6},{8,9},{9,8},{10,11... | collective-permute-start | bytes 1204232 | tf_op jit(solution)/shard_map/ppermute | solution.py:388
  158.3 16.2 %collective-permute-start.48 = (bf16[32,6272]{1,0:T(8,128)(2,1)}, bf16[32,6272]{1,0:T(8,128)(2,1)S(1)}, u32[]{:S(2)}, u32[]{:S(2)}) collective-permute-start(bf16[32,6272]{1,0:T(8,128)(2,1)} %get-tuple-element.137), channel_id=1, source_target_pairs={{0,1},{1,0},{2,3},{3,2},{4,5},{5,4},{6,7},{7,6},{8,9},{9,8},{10,11... | collective-permute-start | bytes 1204232 | tf_op jit(solution)/shard_map/ppermute | solution.py:388
  161.9 20.3 %collective-permute-start.49 = (bf16[64,6144]{1,0:T(8,128)(2,1)}, bf16[64,6144]{1,0:T(8,128)(2,1)}, u32[]{:S(2)}, u32[]{:S(2)}) collective-permute-start(bf16[64,6144]{1,0:T(8,128)(2,1)} %shard_map.119), channel_id=1, source_target_pairs={{0,2},{2,0},{1,3},{3,1},{4,6},{6,4},{5,7},{7,5},{8,10},{10,8},{9,1... | collective-permute-start | bytes 2359304 | tf_op jit(solution)/shard_map/ppermute | solution.py:396
  191.4 5.5 %collective-permute-start.54 = (f32[2,4,256]{2,1,0:T(4,128)S(1)}, f32[2,4,256]{2,1,0:T(4,128)S(1)}, u32[]{:S(2)}, u32[]{:S(2)}) collective-permute-start(f32[2,4,256]{2,1,0:T(4,128)S(1)} %get-tuple-element.149), channel_id=1, source_target_pairs={{0,12},{4,8},{8,4},{12,0},{1,13},{5,9},{9,5},{13,1},{2,14},{6,10},... | collective-permute-start | bytes 24584 | tf_op jit(solution)/shard_map/ppermute | solution.py:369
  (63 other events, 395.6 us)
where the time goes:
time: 201 us
  Pallas kernels  112 us (56%)
  starting transfers between devices  43.2 us (21%)
  waiting for transfers between devices  35.2 us (18%)
  local copies, waits for them, and re-layouts  7.83 us (4%)
    pallas_call x8, Pallas kernels, partial_product(): pl.pallas_call(functools.partial(partial_kernel, contract, tile), in_spec...  88.2 us
    ppermute x13, starting transfers between devices, hop(): return lax.ppermute(a, 'row', pairs)  22.6 us
    pallas_call x3, Pallas kernels, side_call(): pl.pallas_call(kernel, in_specs=[anywhere] * len(terms) + [vmem if v else...  15.9 us
    ppermute x32, waiting for transfers between devices, product(): lax.ppermute(send, 'col', SIBLING)  10.9 us
    ppermute x8, starting transfers between devices, combine(): far.append(lax.ppermute(outs[i][0], 'col', ACROSS))  10.9 us
    ppermute x8, waiting for transfers between devices, combine(): far.append(lax.ppermute(outs[i][0], 'col', ACROSS))  10.8 us
    ppermute x13, waiting for transfers between devices, hop(): return lax.ppermute(a, 'row', pairs)  9.83 us
    pallas_call x8, Pallas kernels, add_rows(): pl.pallas_call(add_kernel, in_specs=[pl.BlockSpec(memory_space=pl.ANY)] *...  7.86 us
  transfers between devices with their start and end apart: 55, of which 26 were waited for; matrix products, arithmetic and copies ran while one was open for 1% of the time, Pallas kernels for 54%

commit v1 on v0

--- a/solution.py
+++ b/solution.py
@@ -79,8 +79,8 @@
         rows, y_ref, w_v, row_sem, w_sem, out_sem = refs
     tiles = w_ref.shape[1 - contract] // tile
     quarter = rows.shape[0] // 4
-    piece = 2 * quarter // PIECES
-    parts = [(n * piece, piece, ref) for n, ref in enumerate(send_refs)]
+    firsts = [sum(SHARES[:n]) * quarter // 2 for n in range(PIECES)]
+    parts = [(first, ref.shape[0], ref) for first, ref in zip(firsts, send_refs)]
     parts += [(2 * quarter, quarter, fwd_ref), (3 * quarter, quarter, keep_ref)]
 
     def row_copies(source, target, sem):
@@ -176,7 +176,8 @@
 COST = 4.8e9
 ECOST = 2.6e9
 AHEAD = 3
-PIECES = 4
+SHARES = (1, 1, 2)
+PIECES = len(SHARES)
 
 
 def in_hbm(*arrays):
@@ -206,7 +207,7 @@
         functools.partial(partial_kernel, contract, tile),
         in_specs=[scalars, scalars] + [anywhere] * len(ins),
         out_specs=[anywhere] * (PIECES + 2),
-        out_shape=[pltpu.HBM((2 * quarter // PIECES, width), BF16)] * PIECES
+        out_shape=[pltpu.HBM((share * quarter // 2, width), BF16) for share in SHARES]
         + [pltpu.VMEM((quarter, width), BF16), pltpu.HBM((quarter, width), BF16)],
         scratch_shapes=[
             pltpu.VMEM((tokens, depth), BF16),
@@ -391,8 +392,7 @@
         got = received[i]
         if after is not None:
             got = tie(got, after)
-        half = PIECES // 2
-        outs.append((add_rows(products[i][PIECES], got[:half]), got[half:]))
+        outs.append((add_rows(products[i][PIECES], got[:-1]), got[-1:]))
         far.append(lax.ppermute(outs[i][0], "col", ACROSS))
 
     def terms(i):

time: 201 us -> 197 us (0.980)
    unnamed x81 -> x55, local copies, waits for them, and re-layouts: 6.64 us -> 5.08 us
    ppermute x32 -> x24, starting transfers between devices: 7.8 us -> 6.32 us  [product(): lax.ppermute(send, 'col', SIBLING)]
    ppermute x32 -> x24, waiting for transfers between devices: 10.9 us -> 11.9 us  [product(): lax.ppermute(send, 'col', SIBLING)]
  transfers between devices with their start and end apart: 55 -> 47, of which waited for: 26 -> 23; matrix products, arithmetic and copies ran while one was open for 1% -> 1% of each run, Pallas kernels for 54% -> 55%
where the time goes in v1:
time: 197 us; the launch traced here: 196 us
  Pallas kernels  110 us (56%)
  starting transfers between devices  41.7 us (21%)
  waiting for transfers between devices  35.6 us (18%)
  local copies, waits for them, and re-layouts  6.27 us (3%)
    pallas_call x8, Pallas kernels, partial_product(): pl.pallas_call(functools.partial(partial_kernel, contract, tile), in_spec...  88 us
    ppermute x13, starting transfers between devices, hop(): return lax.ppermute(a, 'row', pairs)  22.5 us
    pallas_call x3, Pallas kernels, side_call(): pl.pallas_call(kernel, in_specs=[anywhere] * len(terms) + [vmem if v else...  16.1 us
    ppermute x24, waiting for transfers between devices, product(): lax.ppermute(send, 'col', SIBLING)  11.9 us
    ppermute x8, starting transfers between devices, combine(): far.append(lax.ppermute(outs[i][0], 'col', ACROSS))  11 us
    ppermute x8, waiting for transfers between devices, combine(): far.append(lax.ppermute(outs[i][0], 'col', ACROSS))  10.5 us
    ppermute x13, waiting for transfers between devices, hop(): return lax.ppermute(a, 'row', pairs)  9.52 us
    ppermute x24, starting transfers between devices, product(): lax.ppermute(send, 'col', SIBLING)  6.32 us
  transfers between devices with their start and end apart: 47, of which 23 were waited for; matrix products, arithmetic and copies ran while one was open for 1% of the time, Pallas kernels for 55%

profile of v1, /device:TPU:0, one launch (start us, length us, event | category | flops | bytes accessed | tf_op | source)
XLA Modules:
  0.0 196.2 jit_solution(8620731453206933102)
XLA Ops:
  0.6 3.1 %collective-permute-start.4 = (bf16[256,1536]{1,0:T(8,128)(2,1)}, bf16[256,1536]{1,0:T(8,128)(2,1)S(1)}, u32[]{:S(2)}, u32[]{:S(2)}) collective-permute-start(bf16[256,1536]{1,0:T(8,128)(2,1)} %refs_1_.2), channel_id=1, source_target_pairs={{0,4},{4,0},{8,12},{12,8},{1,5},{5,1},{9,13},{13,9},{2,6},{6,2},{1... | collective-permute-start | bytes 2359304 | tf_op jit(solution)/shard_map/ppermute | solution.py:370
  4.5 11.3 %shard_map.104 = (bf16[32,6272]{1,0:T(8,128)(2,1)}, bf16[32,6272]{1,0:T(8,128)(2,1)}, bf16[64,6272]{1,0:T(8,128)(2,1)}, bf16[64,6272]{1,0:T(8,128)(2,1)S(1)}, bf16[64,6272]{1,0:T(8,128)(2,1)}) custom-call(s32[1]{0:T(128)} %constant.67.clone.1.pick_ref, s32[4]{0:T(128)S(1)} %pad_add_fusion.order_ref, bf16[256,1536]{1,0:T(8,128)(2,1)} %refs_1_.2, ...), custom_call_target="tpu_custom_call" | custom-call | flops 4800000000 | bytes 1000 | tf_op jit(solution)/shard_map/pallas_call | solution.py:206
  16.4 4.4 %collective-permute-start.10 = (bf16[256,1536]{1,0:T(8,128)(2,1)S(1)}, bf16[256,1536]{1,0:T(8,128)(2,1)S(1)}, u32[]{:S(2)}, u32[]{:S(2)}) collective-permute-start(bf16[256,1536]{1,0:T(8,128)(2,1)S(1)} %copy-done.8), channel_id=1, source_target_pairs={{0,4},{4,0},{8,12},{12,8},{1,5},{5,1},{9,13},{13,9},{2,6},{6,2},{1... | collective-permute-start | bytes 2359304 | tf_op jit(solution)/shard_map/ppermute | solution.py:370
  20.8 1.6 collective-permute-start.11
  23.0 1.6 collective-permute-start.2
  24.6 10.2 %shard_map.106 = (bf16[32,6144]{1,0:T(8,128)(2,1)}, bf16[32,6144]{1,0:T(8,128)(2,1)}, bf16[64,6144]{1,0:T(8,128)(2,1)}, bf16[64,6144]{1,0:T(8,128)(2,1)S(1)}, bf16[64,6144]{1,0:T(8,128)(2,1)}) custom-call(s32[1]{0:T(128)} %constant.67.clone.1.pick_ref, s32[4]{0:T(128)S(1)} %pad_add_fusion.order_ref, bf16[256,1536]{1,0:T(8,128)(2,1)} %refs_1_.3, ...), custom_call_target="tpu_custom_call" | custom-call | flops 4800000000 | bytes 1000 | tf_op jit(solution)/shard_map/pallas_call | solution.py:206
  40.1 2.9 %collective-permute-done.2.refs_1_ = bf16[64,6272]{1,0:T(8,128)(2,1)S(1)} collective-permute-done((bf16[64,6272]{1,0:T(8,128)(2,1)S(1)}, bf16[64,6272]{1,0:T(8,128)(2,1)S(1)}, u32[]{:S(2)}, u32[]{:S(2)}) %collective-permute-start.2) | collective-permute-done | bytes 802848 | tf_op jit(solution)/shard_map/ppermute | solution.py:396
  43.0 11.3 %shard_map.108 = (bf16[32,6272]{1,0:T(8,128)(2,1)}, bf16[32,6272]{1,0:T(8,128)(2,1)}, bf16[64,6272]{1,0:T(8,128)(2,1)}, bf16[64,6272]{1,0:T(8,128)(2,1)S(1)}, bf16[64,6272]{1,0:T(8,128)(2,1)}) custom-call(s32[1]{0:T(128)} %constant.67.clone.1.pick_ref, s32[4]{0:T(128)S(1)} %pad_add_fusion.order_ref, bf16[256,1536]{1,0:T(8,128)(2,1)} %copy-done.10, ...), custom_call_target="tpu_custom_call" | custom-call | flops 4800000000 | bytes 1000 | tf_op jit(solution)/shard_map/pallas_call | solution.py:206
  57.6 1.6 collective-permute-start.23
  59.9 1.9 collective-permute-done.16.refs_1_
  61.7 1.5 collective-permute-start.14
  63.3 10.2 %shard_map.110 = (bf16[32,6144]{1,0:T(8,128)(2,1)}, bf16[32,6144]{1,0:T(8,128)(2,1)}, bf16[64,6144]{1,0:T(8,128)(2,1)}, bf16[64,6144]{1,0:T(8,128)(2,1)S(1)}, bf16[64,6144]{1,0:T(8,128)(2,1)}) custom-call(s32[1]{0:T(128)} %constant.67.clone.1.pick_ref, s32[4]{0:T(128)S(1)} %pad_add_fusion.order_ref, bf16[256,1536]{1,0:T(8,128)(2,1)} %copy-done.9, ...), custom_call_target="tpu_custom_call" | custom-call | flops 4800000000 | bytes 1000 | tf_op jit(solution)/shard_map/pallas_call | solution.py:206
  79.3 2.2 %collective-permute-done.14.refs_7_ = bf16[64,6272]{1,0:T(8,128)(2,1)} collective-permute-done((bf16[64,6272]{1,0:T(8,128)(2,1)S(1)}, bf16[64,6272]{1,0:T(8,128)(2,1)}, u32[]{:S(2)}, u32[]{:S(2)}) %collective-permute-start.14) | collective-permute-done | bytes 802848 | tf_op jit(solution)/shard_map/ppermute | solution.py:396
  81.5 11.4 %shard_map.112 = (bf16[32,6272]{1,0:T(8,128)(2,1)}, bf16[32,6272]{1,0:T(8,128)(2,1)}, bf16[64,6272]{1,0:T(8,128)(2,1)}, bf16[64,6272]{1,0:T(8,128)(2,1)S(1)}, bf16[64,6272]{1,0:T(8,128)(2,1)}) custom-call(s32[1]{0:T(128)} %bitcast.6.pick_ref, s32[4]{0:T(128)S(1)} %pad_add_fusion.order_ref, bf16[256,1536]{1,0:T(8,128)(2,1)} %copy-done.20, ...), custom_call_target="tpu_custom_call" | custom-call | flops 4800000000 | bytes 1000 | tf_op jit(solution)/shard_map/pallas_call | solution.py:206
  96.1 2.5 %collective-permute-start.26 = (bf16[64,6272]{1,0:T(8,128)(2,1)S(1)}, bf16[64,6272]{1,0:T(8,128)(2,1)S(1)}, u32[]{:S(2)}, u32[]{:S(2)}) collective-permute-start(bf16[64,6272]{1,0:T(8,128)(2,1)S(1)} %shard_map.113), channel_id=1, source_target_pairs={{0,2},{2,0},{1,3},{3,1},{4,6},{6,4},{5,7},{7,5},{8,10},{10,8},{9,1... | collective-permute-start | bytes 2408456 | tf_op jit(solution)/shard_map/ppermute | solution.py:396
  98.7 11.0 %shard_map.114 = (bf16[32,6144]{1,0:T(8,128)(2,1)}, bf16[32,6144]{1,0:T(8,128)(2,1)}, bf16[64,6144]{1,0:T(8,128)(2,1)}, bf16[64,6144]{1,0:T(8,128)(2,1)S(1)}, bf16[64,6144]{1,0:T(8,128)(2,1)}) custom-call(s32[1]{0:T(128)} %bitcast.6.pick_ref, s32[4]{0:T(128)S(1)} %pad_add_fusion.order_ref, bf16[256,1536]{1,0:T(8,128)(2,1)} %collective-permute-done.11.refs_2_.refs_0_, ...), custom_call_target="tpu_custom_call" | custom-call | flops 4800000000 | bytes 1000 | tf_op jit(solution)/shard_map/pallas_call | solution.py:206
  113.5 3.3 %collective-permute-done.33.refs_3_.refs_1_ = bf16[256,1536]{1,0:T(8,128)(2,1)S(1)} collective-permute-done((bf16[256,1536]{1,0:T(8,128)(2,1)}, bf16[256,1536]{1,0:T(8,128)(2,1)S(1)}, u32[]{:S(2)}, u32[]{:S(2)}) %collective-permute-start.33) | collective-permute-done | bytes 786464 | tf_op jit(solution)/shard_map/ppermute | solution.py:370
  117.6 11.4 %shard_map.116 = (bf16[32,6272]{1,0:T(8,128)(2,1)}, bf16[32,6272]{1,0:T(8,128)(2,1)}, bf16[64,6272]{1,0:T(8,128)(2,1)}, bf16[64,6272]{1,0:T(8,128)(2,1)S(1)}, bf16[64,6272]{1,0:T(8,128)(2,1)}) custom-call(s32[1]{0:T(128)} %bitcast.6.pick_ref, s32[4]{0:T(128)S(1)} %pad_add_fusion.order_ref, bf16[256,1536]{1,0:T(8,128)(2,1)} %copy-done.19, ...), custom_call_target="tpu_custom_call" | custom-call | flops 4800000000 | bytes 1000 | tf_op jit(solution)/shard_map/pallas_call | solution.py:206
  132.9 1.8 collective-permute-start.39
  134.7 11.2 %shard_map.118 = (bf16[32,6144]{1,0:T(8,128)(2,1)}, bf16[32,6144]{1,0:T(8,128)(2,1)}, bf16[64,6144]{1,0:T(8,128)(2,1)}, bf16[64,6144]{1,0:T(8,128)(2,1)S(1)}, bf16[64,6144]{1,0:T(8,128)(2,1)}) custom-call(s32[1]{0:T(128)} %bitcast.6.pick_ref, s32[4]{0:T(128)S(1)} %pad_add_fusion.order_ref, bf16[256,1536]{1,0:T(8,128)(2,1)} %collective-permute-done.23.refs_2_.refs_0_, ...), custom_call_target="tpu_custom_call" | custom-call | flops 4800000000 | bytes 1000 | tf_op jit(solution)/shard_map/pallas_call | solution.py:206
  147.9 2.2 %collective-permute-done.36.refs_0_ = bf16[32,6144]{1,0:T(8,128)(2,1)S(1)} collective-permute-done((bf16[32,6144]{1,0:T(8,128)(2,1)}, bf16[32,6144]{1,0:T(8,128)(2,1)S(1)}, u32[]{:S(2)}, u32[]{:S(2)}) %collective-permute-start.36) | collective-permute-done | bytes 393248 | tf_op jit(solution)/shard_map/ppermute | solution.py:389
  156.1 1.5 shard_map.119
  157.7 1.8 collective-permute-start.41
  159.5 9.7 %shard_map.120 = (f32[192,64]{1,0:T(8,128)S(1)}, f32[192,64]{1,0:T(8,128)S(1)}, f32[192,128]{1,0:T(8,128)S(1)}, bf16[64,6144]{1,0:T(8,128)(2,1)S(1)}, bf16[64,6144]{1,0:T(8,128)(2,1)S(1)}) custom-call(bf16[64,6272]{1,0:T(8,128)(2,1)} %get-tuple-element.66.refs_0_, bf16[64,6272]{1,0:T(8,128)(2,1)} %copy-done.12, bf16[64,6272]{1,0:T(8,128)(2,1)} %copy-done.14, ...), custom_call_target="tpu_custom_call" | custom-call | flops 1000 | bytes 1000 | tf_op jit(solution)/shard_map/pallas_call | solution.py:345
  169.2 3.6 %shard_map.121 = (f32[64,64]{1,0:T(8,128)S(1)}, f32[64,6144]{1,0:T(8,128)S(1)}, f32[64,128]{1,0:T(8,128)S(1)}) custom-call(bf16[64,6272]{1,0:T(8,128)(2,1)} %get-tuple-element.119.refs_0_, bf16[64,6272]{1,0:T(8,128)(2,1)} %copy-done.25, bf16[64,6272]{1,0:T(8,128)(2,1)} %collective-permute-done.40.refs_2_, bf16[64,6144]{1,0:T(8,128)(2,1)S(1)} %get-tuple-element.121.refs_3_), custom_call_target="tpu_custom_call" | custom-call | flops 2600000000 | bytes 1000 | tf_op jit(solution)/shard_map/pallas_call | solution.py:345
  173.7 4.3 %collective-permute-done.41.refs_1_ = bf16[64,6144]{1,0:T(8,128)(2,1)} collective-permute-done((bf16[64,6144]{1,0:T(8,128)(2,1)}, bf16[64,6144]{1,0:T(8,128)(2,1)}, u32[]{:S(2)}, u32[]{:S(2)}) %collective-permute-start.41) | collective-permute-done | bytes 786464 | tf_op jit(solution)/shard_map/ppermute | solution.py:396
  178.0 2.8 %shard_map.122 = f32[64,64]{1,0:T(8,128)S(1)} custom-call(bf16[64,6144]{1,0:T(8,128)(2,1)} %get-tuple-element.124.refs_0_, bf16[64,6144]{1,0:T(8,128)(2,1)} %collective-permute-done.41.refs_1_, bf16[64,6144]{1,0:T(8,128)(2,1)} %collective-permute-done.38.refs_2_, f32[64,6144]{1,0:T(8,128)S(1)} %get-tuple-element.126.refs_3_, bf16[64,6144]{1,0:T(8,128)(2,1)S(1)} %copy-done.3), custom_call_target="tpu_custom_call" | custom-call | flops 1000 | bytes 1000 | tf_op jit(solution)/shard_map/pallas_call | solution.py:345
  181.5 1.8 collective-permute-start.42
  183.3 2.5 %collective-permute-done.42 = f32[4,2,2,4,256]{4,3,2,1,0:T(4,128)S(1)} collective-permute-done((f32[4,2,2,4,256]{4,3,2,1,0:T(4,128)S(1)}, f32[4,2,2,4,256]{4,3,2,1,0:T(4,128)S(1)}, u32[]{:S(2)}, u32[]{:S(2)}) %collective-permute-start.42) | collective-permute-done | bytes 65568 | tf_op jit(solution)/shard_map/ppermute | solution.py:482
  187.1 2.9 %collective-permute-start.46 = (f32[2,4,256]{2,1,0:T(4,128)S(1)}, f32[2,4,256]{2,1,0:T(4,128)S(1)}, u32[]{:S(2)}, u32[]{:S(2)}) collective-permute-start(f32[2,4,256]{2,1,0:T(4,128)S(1)} %get-tuple-element.131), channel_id=1, source_target_pairs={{0,12},{4,8},{8,4},{12,0},{1,13},{5,9},{9,5},{13,1},{2,14},{6,10},... | collective-permute-start | bytes 24584 | tf_op jit(solution)/shard_map/ppermute | solution.py:370
  190.0 1.9 collective-permute-start.45
  192.7 1.9 collective-permute-done.45
  (159 shorter events, 41.8 us)
Async XLA Ops:
  0.6 23.9 %collective-permute-start.4 = (bf16[256,1536]{1,0:T(8,128)(2,1)}, bf16[256,1536]{1,0:T(8,128)(2,1)S(1)}, u32[]{:S(2)}, u32[]{:S(2)}) collective-permute-start(bf16[256,1536]{1,0:T(8,128)(2,1)} %refs_1_.2), channel_id=1, source_target_pairs={{0,4},{4,0},{8,12},{12,8},{1,5},{5,1},{9,13},{13,9},{2,6},{6,2},{1... | collective-permute-start | bytes 2359304 | tf_op jit(solution)/shard_map/ppermute | solution.py:370
  3.7 20.9 %collective-permute-start.5 = (bf16[256,1536]{1,0:T(8,128)(2,1)}, bf16[256,1536]{1,0:T(8,128)(2,1)S(1)}, u32[]{:S(2)}, u32[]{:S(2)}) collective-permute-start(bf16[256,1536]{1,0:T(8,128)(2,1)} %refs_1_.2), channel_id=1, source_target_pairs={{4,8},{8,4},{5,9},{9,5},{6,10},{10,6},{7,11},{11,7},{20,24},{24,20... | collective-permute-start | bytes 2359304 | tf_op jit(solution)/shard_map/ppermute | solution.py:370
  15.8 4.9 %collective-permute-start = (bf16[32,6272]{1,0:T(8,128)(2,1)}, bf16[32,6272]{1,0:T(8,128)(2,1)S(1)}, u32[]{:S(2)}, u32[]{:S(2)}) collective-permute-start(bf16[32,6272]{1,0:T(8,128)(2,1)} %get-tuple-element.68), channel_id=1, source_target_pairs={{0,1},{1,0},{2,3},{3,2},{4,5},{5,4},{6,7},{7,6},{8,9},{9,8},{10,11... | collective-permute-start | bytes 1204232 | tf_op jit(solution)/shard_map/ppermute | solution.py:389
  15.9 6.4 %collective-permute-start.1 = (bf16[32,6272]{1,0:T(8,128)(2,1)}, bf16[32,6272]{1,0:T(8,128)(2,1)S(1)}, u32[]{:S(2)}, u32[]{:S(2)}) collective-permute-start(bf16[32,6272]{1,0:T(8,128)(2,1)} %get-tuple-element.69), channel_id=1, source_target_pairs={{0,1},{1,0},{2,3},{3,2},{4,5},{5,4},{6,7},{7,6},{8,9},{9,8},{10,11... | collective-permute-start | bytes 1204232 | tf_op jit(solution)/shard_map/ppermute | solution.py:389
  16.4 23.1 %collective-permute-start.10 = (bf16[256,1536]{1,0:T(8,128)(2,1)S(1)}, bf16[256,1536]{1,0:T(8,128)(2,1)S(1)}, u32[]{:S(2)}, u32[]{:S(2)}) collective-permute-start(bf16[256,1536]{1,0:T(8,128)(2,1)S(1)} %copy-done.8), channel_id=1, source_target_pairs={{0,4},{4,0},{8,12},{12,8},{1,5},{5,1},{9,13},{13,9},{2,6},{6,2},{1... | collective-permute-start | bytes 2359304 | tf_op jit(solution)/shard_map/ppermute | solution.py:370
  20.8 19.3 %collective-permute-start.11 = (bf16[256,1536]{1,0:T(8,128)(2,1)S(1)}, bf16[256,1536]{1,0:T(8,128)(2,1)}, u32[]{:S(2)}, u32[]{:S(2)}) collective-permute-start(bf16[256,1536]{1,0:T(8,128)(2,1)S(1)} %copy-done.8), channel_id=1, source_target_pairs={{4,8},{8,4},{5,9},{9,5},{6,10},{10,6},{7,11},{11,7},{20,24},{24,20... | collective-permute-start | bytes 2359304 | tf_op jit(solution)/shard_map/ppermute | solution.py:370
  23.0 20.0 %collective-permute-start.2 = (bf16[64,6272]{1,0:T(8,128)(2,1)S(1)}, bf16[64,6272]{1,0:T(8,128)(2,1)S(1)}, u32[]{:S(2)}, u32[]{:S(2)}) collective-permute-start(bf16[64,6272]{1,0:T(8,128)(2,1)S(1)} %shard_map.105), channel_id=1, source_target_pairs={{0,2},{2,0},{1,3},{3,1},{4,6},{6,4},{5,7},{7,5},{8,10},{10,8},{9,1... | collective-permute-start | bytes 2408456 | tf_op jit(solution)/shard_map/ppermute | solution.py:396
  36.8 26.4 %collective-permute-start.17 = (bf16[256,1536]{1,0:T(8,128)(2,1)S(1)}, bf16[256,1536]{1,0:T(8,128)(2,1)S(1)}, u32[]{:S(2)}, u32[]{:S(2)}) collective-permute-start(bf16[256,1536]{1,0:T(8,128)(2,1)S(1)} %collective-permute-done.4.refs_0_.refs_1_), channel_id=1, source_target_pairs={{4,8},{8,4},{5,9},{9,5},{6,10},{10,6},{7,11},{11,7},{20,24},{24,20... | collective-permute-start | bytes 2359304 | tf_op jit(solution)/shard_map/ppermute | solution.py:370
  37.5 24.2 %collective-permute-start.16 = (bf16[256,1536]{1,0:T(8,128)(2,1)S(1)}, bf16[256,1536]{1,0:T(8,128)(2,1)S(1)}, u32[]{:S(2)}, u32[]{:S(2)}) collective-permute-start(bf16[256,1536]{1,0:T(8,128)(2,1)S(1)} %collective-permute-done.5.refs_0_), channel_id=1, source_target_pairs={{4,0},{8,12},{5,1},{9,13},{6,2},{10,14},{7,3},{11,15},{20,16},{24,... | collective-permute-start | bytes 2359304 | tf_op jit(solution)/shard_map/ppermute | solution.py:370
  39.5 23.7 %collective-permute-start.8 = (bf16[64,6144]{1,0:T(8,128)(2,1)S(1)}, bf16[64,6144]{1,0:T(8,128)(2,1)S(1)}, u32[]{:S(2)}, u32[]{:S(2)}) collective-permute-start(bf16[64,6144]{1,0:T(8,128)(2,1)S(1)} %shard_map.107), channel_id=1, source_target_pairs={{0,2},{2,0},{1,3},{3,1},{4,6},{6,4},{5,7},{7,5},{8,10},{10,8},{9,1... | collective-permute-start | bytes 2359304 | tf_op jit(solution)/shard_map/ppermute | solution.py:396
  56.3 22.9 %collective-permute-start.22 = (bf16[256,1536]{1,0:T(8,128)(2,1)}, bf16[256,1536]{1,0:T(8,128)(2,1)}, u32[]{:S(2)}, u32[]{:S(2)}) collective-permute-start(bf16[256,1536]{1,0:T(8,128)(2,1)} %collective-permute-done.11.refs_2_.refs_0_), channel_id=1, source_target_pairs={{4,0},{8,12},{5,1},{9,13},{6,2},{10,14},{7,3},{11,15},{20,16},{24,... | collective-permute-start | bytes 2359304 | tf_op jit(solution)/shard_map/ppermute | solution.py:370
  57.6 21.6 %collective-permute-start.23 = (bf16[256,1536]{1,0:T(8,128)(2,1)}, bf16[256,1536]{1,0:T(8,128)(2,1)}, u32[]{:S(2)}, u32[]{:S(2)}) collective-permute-start(bf16[256,1536]{1,0:T(8,128)(2,1)} %copy-done.9), channel_id=1, source_target_pairs={{4,8},{8,4},{5,9},{9,5},{6,10},{10,6},{7,11},{11,7},{20,24},{24,20... | collective-permute-start | bytes 2359304 | tf_op jit(solution)/shard_map/ppermute | solution.py:370
  61.7 19.7 %collective-permute-start.14 = (bf16[64,6272]{1,0:T(8,128)(2,1)S(1)}, bf16[64,6272]{1,0:T(8,128)(2,1)}, u32[]{:S(2)}, u32[]{:S(2)}) collective-permute-start(bf16[64,6272]{1,0:T(8,128)(2,1)S(1)} %shard_map.109), channel_id=1, source_target_pairs={{0,2},{2,0},{1,3},{3,1},{4,6},{6,4},{5,7},{7,5},{8,10},{10,8},{9,1... | collective-permute-start | bytes 2408456 | tf_op jit(solution)/shard_map/ppermute | solution.py:396
  75.5 23.1 %collective-permute-start.28 = (bf16[256,1536]{1,0:T(8,128)(2,1)S(1)}, bf16[256,1536]{1,0:T(8,128)(2,1)S(1)}, u32[]{:S(2)}, u32[]{:S(2)}) collective-permute-start(bf16[256,1536]{1,0:T(8,128)(2,1)S(1)} %collective-permute-done.17.refs_0_), channel_id=1, source_target_pairs={{4,0},{8,12},{5,1},{9,13},{6,2},{10,14},{7,3},{11,15},{20,16},{24,... | collective-permute-start | bytes 2359304 | tf_op jit(solution)/shard_map/ppermute | solution.py:370
  77.5 21.2 %collective-permute-start.20 = (bf16[64,6144]{1,0:T(8,128)(2,1)S(1)}, bf16[64,6144]{1,0:T(8,128)(2,1)S(1)}, u32[]{:S(2)}, u32[]{:S(2)}) collective-permute-start(bf16[64,6144]{1,0:T(8,128)(2,1)S(1)} %shard_map.111), channel_id=1, source_target_pairs={{0,2},{2,0},{1,3},{3,1},{4,6},{6,4},{5,7},{7,5},{8,10},{10,8},{9,1... | collective-permute-start | bytes 2359304 | tf_op jit(solution)/shard_map/ppermute | solution.py:396
  93.4 23.3 %collective-permute-start.33 = (bf16[256,1536]{1,0:T(8,128)(2,1)}, bf16[256,1536]{1,0:T(8,128)(2,1)S(1)}, u32[]{:S(2)}, u32[]{:S(2)}) collective-permute-start(bf16[256,1536]{1,0:T(8,128)(2,1)} %collective-permute-done.23.refs_2_.refs_0_), channel_id=1, source_target_pairs={{4,0},{8,12},{5,1},{9,13},{6,2},{10,14},{7,3},{11,15},{20,16},{24,... | collective-permute-start | bytes 2359304 | tf_op jit(solution)/shard_map/ppermute | solution.py:370
  96.1 21.2 %collective-permute-start.26 = (bf16[64,6272]{1,0:T(8,128)(2,1)S(1)}, bf16[64,6272]{1,0:T(8,128)(2,1)S(1)}, u32[]{:S(2)}, u32[]{:S(2)}) collective-permute-start(bf16[64,6272]{1,0:T(8,128)(2,1)S(1)} %shard_map.113), channel_id=1, source_target_pairs={{0,2},{2,0},{1,3},{3,1},{4,6},{6,4},{5,7},{7,5},{8,10},{10,8},{9,1... | collective-permute-start | bytes 2408456 | tf_op jit(solution)/shard_map/ppermute | solution.py:396
  112.9 21.8 %collective-permute-start.31 = (bf16[64,6144]{1,0:T(8,128)(2,1)S(1)}, bf16[64,6144]{1,0:T(8,128)(2,1)S(1)}, u32[]{:S(2)}, u32[]{:S(2)}) collective-permute-start(bf16[64,6144]{1,0:T(8,128)(2,1)S(1)} %shard_map.115), channel_id=1, source_target_pairs={{0,2},{2,0},{1,3},{3,1},{4,6},{6,4},{5,7},{7,5},{8,10},{10,8},{9,1... | collective-permute-start | bytes 2359304 | tf_op jit(solution)/shard_map/ppermute | solution.py:396
  129.6 17.7 %collective-permute-start.3 = (bf16[64,6272]{1,0:T(8,128)(2,1)S(1)}, bf16[64,6272]{1,0:T(8,128)(2,1)S(1)}, u32[]{:S(2)}, u32[]{:S(2)}) collective-permute-start(bf16[64,6272]{1,0:T(8,128)(2,1)S(1)} %copy-done.24), channel_id=1, source_target_pairs={{0,1},{1,0},{2,3},{3,2},{4,5},{5,4},{6,7},{7,6},{8,9},{9,8},{10,11... | collective-permute-start | bytes 2408456 | tf_op jit(solution)/shard_map/ppermute | solution.py:389
  129.7 17.7 %collective-permute-start.9 = (bf16[64,6144]{1,0:T(8,128)(2,1)S(1)}, bf16[64,6144]{1,0:T(8,128)(2,1)S(1)}, u32[]{:S(2)}, u32[]{:S(2)}) collective-permute-start(bf16[64,6144]{1,0:T(8,128)(2,1)S(1)} %copy-done.26), channel_id=1, source_target_pairs={{0,1},{1,0},{2,3},{3,2},{4,5},{5,4},{6,7},{7,6},{8,9},{9,8},{10,11... | collective-permute-start | bytes 2359304 | tf_op jit(solution)/shard_map/ppermute | solution.py:389
  132.9 20.0 %collective-permute-start.39 = (bf16[64,6272]{1,0:T(8,128)(2,1)S(1)}, bf16[64,6272]{1,0:T(8,128)(2,1)S(1)}, u32[]{:S(2)}, u32[]{:S(2)}) collective-permute-start(bf16[64,6272]{1,0:T(8,128)(2,1)S(1)} %shard_map.117), channel_id=1, source_target_pairs={{0,2},{2,0},{1,3},{3,1},{4,6},{6,4},{5,7},{7,5},{8,10},{10,8},{9,1... | collective-permute-start | bytes 2408456 | tf_op jit(solution)/shard_map/ppermute | solution.py:396
  146.8 7.0 %collective-permute-start.38 = (bf16[64,6144]{1,0:T(8,128)(2,1)}, bf16[64,6144]{1,0:T(8,128)(2,1)}, u32[]{:S(2)}, u32[]{:S(2)}) collective-permute-start(bf16[64,6144]{1,0:T(8,128)(2,1)} %get-tuple-element.113), channel_id=1, source_target_pairs={{0,1},{1,0},{2,3},{3,2},{4,5},{5,4},{6,7},{7,6},{8,9},{9,8},{10,11... | collective-permute-start | bytes 2359304 | tf_op jit(solution)/shard_map/ppermute | solution.py:389
  147.3 3.9 %collective-permute-start.37 = (bf16[32,6144]{1,0:T(8,128)(2,1)}, bf16[32,6144]{1,0:T(8,128)(2,1)S(1)}, u32[]{:S(2)}, u32[]{:S(2)}) collective-permute-start(bf16[32,6144]{1,0:T(8,128)(2,1)} %get-tuple-element.112), channel_id=1, source_target_pairs={{0,1},{1,0},{2,3},{3,2},{4,5},{5,4},{6,7},{7,6},{8,9},{9,8},{10,11... | collective-permute-start | bytes 1179656 | tf_op jit(solution)/shard_map/ppermute | solution.py:389
  147.4 10.3 %collective-permute-start.15 = (bf16[64,6272]{1,0:T(8,128)(2,1)}, bf16[64,6272]{1,0:T(8,128)(2,1)}, u32[]{:S(2)}, u32[]{:S(2)}) collective-permute-start(bf16[64,6272]{1,0:T(8,128)(2,1)} %get-tuple-element.82), channel_id=1, source_target_pairs={{0,1},{1,0},{2,3},{3,2},{4,5},{5,4},{6,7},{7,6},{8,9},{9,8},{10,11... | collective-permute-start | bytes 2408456 | tf_op jit(solution)/shard_map/ppermute | solution.py:389
  150.1 9.4 %collective-permute-start.27 = (bf16[64,6272]{1,0:T(8,128)(2,1)}, bf16[64,6272]{1,0:T(8,128)(2,1)}, u32[]{:S(2)}, u32[]{:S(2)}) collective-permute-start(bf16[64,6272]{1,0:T(8,128)(2,1)} %get-tuple-element.96), channel_id=1, source_target_pairs={{0,1},{1,0},{2,3},{3,2},{4,5},{5,4},{6,7},{7,6},{8,9},{9,8},{10,11... | collective-permute-start | bytes 2408456 | tf_op jit(solution)/shard_map/ppermute | solution.py:389
  152.0 17.2 %collective-permute-start.40 = (bf16[64,6272]{1,0:T(8,128)(2,1)}, bf16[64,6272]{1,0:T(8,128)(2,1)}, u32[]{:S(2)}, u32[]{:S(2)}) collective-permute-start(bf16[64,6272]{1,0:T(8,128)(2,1)} %get-tuple-element.120), channel_id=1, source_target_pairs={{0,1},{1,0},{2,3},{3,2},{4,5},{5,4},{6,7},{7,6},{8,9},{9,8},{10,11... | collective-permute-start | bytes 2408456 | tf_op jit(solution)/shard_map/ppermute | solution.py:389
  152.9 6.6 %collective-permute-start.21 = (bf16[64,6144]{1,0:T(8,128)(2,1)}, bf16[64,6144]{1,0:T(8,128)(2,1)}, u32[]{:S(2)}, u32[]{:S(2)}) collective-permute-start(bf16[64,6144]{1,0:T(8,128)(2,1)} %get-tuple-element.89), channel_id=1, source_target_pairs={{0,1},{1,0},{2,3},{3,2},{4,5},{5,4},{6,7},{7,6},{8,9},{9,8},{10,11... | collective-permute-start | bytes 2359304 | tf_op jit(solution)/shard_map/ppermute | solution.py:389
  153.8 5.7 %collective-permute-start.32 = (bf16[64,6144]{1,0:T(8,128)(2,1)}, bf16[64,6144]{1,0:T(8,128)(2,1)}, u32[]{:S(2)}, u32[]{:S(2)}) collective-permute-start(bf16[64,6144]{1,0:T(8,128)(2,1)} %get-tuple-element.103), channel_id=1, source_target_pairs={{0,1},{1,0},{2,3},{3,2},{4,5},{5,4},{6,7},{7,6},{8,9},{9,8},{10,11... | collective-permute-start | bytes 2359304 | tf_op jit(solution)/shard_map/ppermute | solution.py:389
  157.7 20.3 %collective-permute-start.41 = (bf16[64,6144]{1,0:T(8,128)(2,1)}, bf16[64,6144]{1,0:T(8,128)(2,1)}, u32[]{:S(2)}, u32[]{:S(2)}) collective-permute-start(bf16[64,6144]{1,0:T(8,128)(2,1)} %shard_map.119), channel_id=1, source_target_pairs={{0,2},{2,0},{1,3},{3,1},{4,6},{6,4},{5,7},{7,5},{8,10},{10,8},{9,1... | collective-permute-start | bytes 2359304 | tf_op jit(solution)/shard_map/ppermute | solution.py:396
  181.5 4.3 %collective-permute-start.42 = (f32[4,2,2,4,256]{4,3,2,1,0:T(4,128)S(1)}, f32[4,2,2,4,256]{4,3,2,1,0:T(4,128)S(1)}, u32[]{:S(2)}, u32[]{:S(2)}) collective-permute-start(f32[4,2,2,4,256]{4,3,2,1,0:T(4,128)S(1)} %dynamic-slice_bitcast_fusion), channel_id=1, source_target_pairs={{0,2},{2,0},{1,3},{3,1},{4,6},{6,4},{5,7},{7,5},{8,10},{10,8},{9,1... | collective-permute-start | bytes 196616 | tf_op jit(solution)/shard_map/ppermute | solution.py:482
  187.1 5.5 %collective-permute-start.46 = (f32[2,4,256]{2,1,0:T(4,128)S(1)}, f32[2,4,256]{2,1,0:T(4,128)S(1)}, u32[]{:S(2)}, u32[]{:S(2)}) collective-permute-start(f32[2,4,256]{2,1,0:T(4,128)S(1)} %get-tuple-element.131), channel_id=1, source_target_pairs={{0,12},{4,8},{8,4},{12,0},{1,13},{5,9},{9,5},{13,1},{2,14},{6,10},... | collective-permute-start | bytes 24584 | tf_op jit(solution)/shard_map/ppermute | solution.py:370
  190.0 4.5 %collective-permute-start.45 = (f32[2,4,256]{2,1,0:T(4,128)S(1)}, f32[2,4,256]{2,1,0:T(4,128)S(1)}, u32[]{:S(2)}, u32[]{:S(2)}) collective-permute-start(f32[2,4,256]{2,1,0:T(4,128)S(1)} %get-tuple-element.132), channel_id=1, source_target_pairs={{0,8},{4,12},{8,0},{12,4},{1,9},{5,13},{9,1},{13,5},{2,10},{6,14},... | collective-permute-start | bytes 24584 | tf_op jit(solution)/shard_map/ppermute | solution.py:370
  (42 other events, 285.6 us)
